TPU v7x, 32 devices: a whole 2x2x4 slice. The times are simulated.
32 devices in a mesh: prow: 8 (over z, y), pcol: 4 (over x, core).
Axes of the slice: x: 2, y: 2, z: 4, core: 2. Of those that a mesh axis runs over, the one named last changes fastest.
Arguments:
- data: float32 [16384, 8192], P('prow', 'pcol'), may hold values from 0.05 to 5
- w_trans: float32 [32, 16384], P(None, ('prow', 'pcol')), as said below
- h_prior: float32 [32, 8192], P(None, 'pcol'), may hold values from 0.1 to 3
Outputs:
- h_next: float32 [32, 8192], P(None, 'pcol')
Inputs may be any that keep to these rules, and one draw needn't show every extreme that they name: `w_trans`: every entry is positive.
All inputs are finite; a program needn't handle non-finite values.
Results may differ from a plain program's by a relative error of at most 0.0003.
Values sent between devices are 32-bit elements; how exact they have to be, the bound alone decides.
No kernel may reach another device: no remote copies, remote signals or barrier semaphores. Data moves between devices by JAX's collectives and lax.ppermute only.
A program may use at most 64 MiB of HBM per device.

v0:
```python
import functools

import jax
import jax.numpy as jnp
from jax import lax
from jax.experimental import pallas as pl
from jax.experimental.pallas import tpu as pltpu
from jax.sharding import PartitionSpec as P

LANES = 128
GRAM_ROWS = 8
VMEM = pl.BlockSpec(memory_space=pltpu.VMEM)
HBM = pl.BlockSpec(memory_space=pltpu.HBM)


def call(kernel, out_shape, operands, name, mebibytes=4, in_specs=None, scratch=(), cost=None,
         out_specs=VMEM):
    many = isinstance(out_shape, list)
    return pl.pallas_call(
        kernel,
        out_shape=out_shape,
        in_specs=in_specs or [VMEM] * len(operands),
        out_specs=[out_specs] * len(out_shape) if many else out_specs,
        compiler_params=pltpu.CompilerParams(vmem_limit_bytes=mebibytes * 1024 * 1024),
        scratch_shapes=list(scratch),
        cost_estimate=cost,
        name=name,
    )(*operands)


def floats(*shape):
    return jax.ShapeDtypeStruct(shape, jnp.float32)


def split(value):
    high = value.astype(jnp.bfloat16)
    low = (value - high.astype(jnp.float32)).astype(jnp.bfloat16)
    return high, low


def exact_dot(left, right, dims):
    return lax.dot_general(
        left, right, (dims, ((), ())),
        precision=lax.Precision.HIGHEST, preferred_element_type=jnp.float32,
    )


def block_start(near, width, side_turn, level_turn):
    row_at = lax.axis_index("prow")
    side, level = lax.rem(row_at, near), lax.div(row_at, near)
    peer = (level ^ level_turn) * near + (side ^ side_turn)
    return pl.multiple_of(peer * width, width)


def row_part(depth, turn):
    return pl.ds(pl.multiple_of((lax.axis_index("pcol") ^ turn) * depth, depth), depth)


def block_copies(near, width, n_col, order, data_ref, out_ref, sems):
    depth = data_ref.shape[0] // n_col
    copies = {}
    for (at, turns), turn in order:
        columns = pl.ds(block_start(near, width, *turns), width)
        rows = row_part(depth, turn)
        copies[at, turn] = pltpu.make_async_copy(
            data_ref.at[rows, columns], out_ref.at[at, rows], sems.at[at, turn]
        )
    return copies


def split_basis(part_ref, out_ref, turn):
    rank = part_ref.shape[0]
    part = part_ref[...]
    high, low = split(part)
    out_ref[turn, :rank] = high
    out_ref[turn, rank:] = low
    return exact_dot(part, part, ((1,), (1,)))


def product(w_split, blocks, at, turns):
    rank, depth = w_split.shape[1] // 2, w_split.shape[2]
    total = None
    for turn in turns:
        high, low = split(blocks[at, row_part(depth, turn)])
        upper = jnp.dot(w_split[turn], high, preferred_element_type=jnp.float32)
        term = (
            upper[:rank]
            + upper[rank:]
            + jnp.dot(w_split[turn, :rank], low, preferred_element_type=jnp.float32)
        )
        total = term if total is None else total + term
    return total


def store(cross, out_ref, row, before=None):
    rank = cross.shape[0]
    for i in range(cross.shape[1] // LANES):
        rows = slice(row + rank * i, row + rank * (i + 1))
        piece = cross[:, LANES * i : LANES * (i + 1)]
        out_ref[rows] = piece if before is None else piece + before[rows]


def own_region(compute):
    pl.when(lax.axis_index("prow") >= 0)(compute)


def load_kernel(near, width, n_col, early, late, others, *refs):
    w_refs, data_ref = refs[: len(early)], refs[len(early)]
    blocks, begun, w_split, gram_ref, sems = refs[len(early) + 1 :]
    order = [(at, turn) for turn in early + late for at in enumerate(others)]
    copies = block_copies(near, width, n_col, order, data_ref, blocks, sems)
    for copy in copies.values():
        copy.start()

    def compute():
        gram = split_basis(w_refs[0], w_split, early[0])
        for turn, ref in list(zip(early, w_refs))[1:]:
            gram = gram + split_basis(ref, w_split, turn)
        gram_ref[...] = gram
        for at in range(len(others)):
            for turn in early:
                copies[at, turn].wait()
            store(product(w_split, blocks, at, early), begun.at[at], 0)

    own_region(compute)
    for (_, turn), copy in copies.items():
        if turn not in early:
            copy.wait()


def other_side_kernel(slab, far, early, late, *refs):
    w_refs, (w_early, gram_early, blocks, begun) = refs[: len(late)], refs[len(late) :][:4]
    *out_refs, w_split, gram_ref = refs[len(late) + 4 :]
    rank = w_refs[0].shape[0]
    for turn in early:
        w_split[turn] = w_early[turn]
    gram = gram_early[...]
    for turn, ref in zip(late, w_refs):
        gram = gram + split_basis(ref, w_split, turn)
    slabs = [gram[GRAM_ROWS * i : GRAM_ROWS * (i + 1)] for i in range(rank // GRAM_ROWS)]
    packed = jnp.concatenate(slabs, axis=1)
    gram_ref[...] = packed
    for index, out_ref in enumerate(out_refs):
        for at in range(far):
            block = index * far + at
            store(
                product(w_split, blocks, block, late), out_ref.at[pl.ds(slab * at, slab)], 0,
                begun.at[block],
            )
        out_ref[slab * far :] = packed


def own_side_kernel(near, width, n_col, owns, w_split, data_ref, out_ref, blocks, sems):
    order = [(at, turn) for at in enumerate(owns) for turn in range(n_col)]
    copies = block_copies(near, width, n_col, order, data_ref, blocks, sems)
    for copy in copies.values():
        copy.start()

    def multiply(at):
        for turn in range(n_col):
            copies[at, turn].wait()
        store(product(w_split, blocks, at, range(n_col)), out_ref.at[at], 0)

    for at in range(len(owns)):
        own_region(functools.partial(multiply, at))


def side_sum_kernel(slab, own_ref, gram_ref, *refs):
    far = own_ref.shape[0]
    got_refs, out_refs = refs[:-far], refs[-far:]
    gram = gram_ref[...]
    for got in got_refs:
        gram = gram + got[slab * far :]
    for at, out_ref in enumerate(out_refs):
        total = own_ref[at]
        for got in got_refs:
            total = total + got[slab * at : slab * (at + 1)]
        out_ref[:slab] = total
        out_ref[slab:] = gram


def sweep_kernel(width, *refs):
    parts, h_ref, out_ref = refs[:-2], refs[-2], refs[-1]
    rank = h_ref.shape[0]
    row_at = lax.axis_index("prow")
    total = parts[0][...]
    for part in parts[1:]:
        total = total + part[...]
    pieces = width // LANES
    cross = jnp.concatenate([total[rank * i : rank * (i + 1)] for i in range(pieces)], axis=1)
    packed = total[rank * pieces :]
    gram = jnp.concatenate(
        [packed[:, rank * i : rank * (i + 1)] for i in range(rank // GRAM_ROWS)], axis=0
    )
    h = h_ref[:, pl.ds(pl.multiple_of(row_at * width, width), width)]
    rest = cross - exact_dot(gram, h, ((1,), (0,)))
    rows = []
    for k in range(rank):
        inverse = 1.0 / gram[k : k + 1, k : k + 1]
        old = h[k : k + 1]
        fresh = jnp.maximum(old + rest[k : k + 1] * inverse, 0.0)
        rows.append(fresh)
        rest = rest - gram[:, k : k + 1] * (fresh - old)
    done = jnp.concatenate(rows, axis=0)
    for peer in range(out_ref.shape[0]):
        out_ref[peer] = done


def assemble_kernel(width, pieces, out_ref, sems):
    copies = []
    for peer in range(pieces.shape[0]):
        columns = pl.ds(width * peer, width)
        copies.append(pltpu.make_async_copy(pieces.at[peer], out_ref.at[:, columns], sems.at[peer]))
        copies[-1].start()
    for copy in copies:
        copy.wait()


def shards(n_row, n_col, data, w_trans, h_prior):
    rank, depth = w_trans.shape
    rows, cols = data.shape
    width = cols // n_row
    near = max(1, n_row // 4)
    far = n_row // near
    slab = rank * (width // LANES)
    turns = [*range(far // 2, far), *range(far // 2 - 1, -1, -1)]
    sides = range(1, near)

    def permute(value, axis, turn):
        size = n_row if axis == "prow" else n_col
        return lax.ppermute(value, axis, [(i, i ^ turn) for i in range(size)])

    w_parts = [w_trans] + [permute(w_trans, "pcol", t) for t in range(1, n_col)]
    early = list(range(1, min(2, n_col)))
    late = [turn for turn in range(n_col) if turn not in early]
    others = [(side, turn) for side in sides for turn in turns]
    owns = [(0, turn) for turn in turns]
    split_parts = jax.ShapeDtypeStruct((n_col, 2 * rank, depth), jnp.bfloat16)
    blocks, begun, w_early, gram_early = call(
        functools.partial(load_kernel, near, width, n_col, early, late, others),
        [
            floats(len(others), rows, width),
            floats(len(others), slab, LANES),
            split_parts,
            floats(rank, rank),
        ],
        [*(w_parts[t] for t in early), data], "load_other_side", 40,
        [VMEM] * len(early) + [HBM], [pltpu.SemaphoreType.DMA((len(others), n_col))],
        pl.CostEstimate(
            flops=0, bytes_accessed=8 * rows * width * len(others), transcendentals=0
        ),
    )
    *sent, w_split, gram = call(
        functools.partial(other_side_kernel, slab, far, early, late),
        [floats(far * slab + GRAM_ROWS, LANES)] * len(sides)
        + [split_parts, floats(GRAM_ROWS, LANES)],
        [*(w_parts[t] for t in late), w_early, gram_early, blocks, begun], "other_side", 8,
    )
    got = [permute(sent[side - 1], "prow", side) for side in sides]
    own = call(
        functools.partial(own_side_kernel, near, width, n_col, owns),
        floats(far, slab, LANES), [w_split, data], "own_side", 40, [VMEM, HBM],
        [
            pltpu.VMEM((far, rows, width), jnp.float32),
            pltpu.SemaphoreType.DMA((far, n_col)),
        ],
    )
    sums = call(
        functools.partial(side_sum_kernel, slab),
        [floats(slab + GRAM_ROWS, LANES)] * far, [own, gram, *got], "side_sum",
    )
    parts = [
        permute(value, "prow", turn * near) if turn else value
        for turn, value in zip(turns, sums)
    ]
    fresh = call(
        functools.partial(sweep_kernel, width), floats(n_row, rank, width),
        [*parts, h_prior], "row_sweep",
    )
    pieces = lax.all_to_all(fresh, "prow", 0, 0)
    return call(
        functools.partial(assemble_kernel, width), floats(rank, cols), [pieces], "assemble",
        scratch=[pltpu.SemaphoreType.DMA((n_row,))], out_specs=HBM,
    )


def solution(mesh):
    n_row, n_col = mesh.shape["prow"], mesh.shape["pcol"]
    placed = (P("prow", "pcol"), P(None, ("prow", "pcol")), P(None, "pcol"))
    return jax.shard_map(
        functools.partial(shards, n_row, n_col),
        mesh=mesh, in_specs=placed, out_specs=P(None, "pcol"), check_vma=False,
    )
```

profile of v0, /device:TPU:0, one launch (start us, length us, event | category | flops | bytes accessed | tf_op | source)
XLA Modules:
  0.0 36.0 jit_solution(11905505424376206303)
XLA Ops:
  0.0 0.0 copy-start.1
  0.0 0.5 %collective-permute-start.2 = (f32[32,512]{1,0:T(8,128)}, f32[32,512]{1,0:T(8,128)S(1)}, u32[]{:S(2)}, u32[]{:S(2)}) collective-permute-start(f32[32,512]{1,0:T(8,128)} %refs_0_.1), channel_id=1, source_target_pairs={{0,1},{1,0},{2,3},{3,2},{4,5},{5,4},{6,7},{7,6},{8,9},{9,8},{10,11... | collective-permute-start | bytes 196616 | tf_op jit(solution)/shard_map/ppermute | solution.py:231
  0.5 2.6 %collective-permute-start.1 = (f32[32,512]{1,0:T(8,128)}, f32[32,512]{1,0:T(8,128)S(1)}, u32[]{:S(2)}, u32[]{:S(2)}) collective-permute-start(f32[32,512]{1,0:T(8,128)} %refs_0_.1), channel_id=1, source_target_pairs={{0,3},{1,2},{2,1},{3,0},{4,7},{5,6},{6,5},{7,4},{8,11},{9,10},{10,... | collective-permute-start | bytes 196616 | tf_op jit(solution)/shard_map/ppermute | solution.py:231
  3.1 0.1 collective-permute-start
  3.1 0.0 collective-permute-done.2.refs_0_
  3.1 3.7 %load_other_side.1 = (f32[4,2048,256]{2,1,0:T(8,128)S(1)}, f32[4,64,128]{2,1,0:T(8,128)S(1)}, bf16[4,64,512]{2,1,0:T(8,128)(2,1)S(1)}, f32[32,32]{1,0:T(8,128)S(1)}) custom-call(f32[32,512]{1,0:T(8,128)S(1)} %collective-permute-done.2.refs_0_, f32[2048,2048]{1,0:T(8,128)} %data_ref.1), custom_call_target="tpu_custom_call" | custom-call | bytes 16777216 | tf_op jit(solution)/shard_map/load_other_side/pallas_call | solution.py:19
  6.8 0.0 copy-start
  6.8 0.0 collective-permute-done.1.refs_2_
  6.9 0.7 %collective-permute-done.refs_1_ = f32[32,512]{1,0:T(8,128)S(1)} collective-permute-done((f32[32,512]{1,0:T(8,128)}, f32[32,512]{1,0:T(8,128)S(1)}, u32[]{:S(2)}, u32[]{:S(2)}) %collective-permute-start) | collective-permute-done | bytes 65568 | tf_op jit(solution)/shard_map/ppermute | solution.py:231
  7.5 0.0 copy-done.1
  7.5 1.4 %other_side.1 = (f32[264,128]{1,0:T(8,128)S(1)}, bf16[4,64,512]{2,1,0:T(8,128)(2,1)S(1)}, f32[8,128]{1,0:T(8,128)S(1)}) custom-call(f32[32,512]{1,0:T(8,128)S(1)} %copy-done.1, f32[32,512]{1,0:T(8,128)S(1)} %collective-permute-done.refs_1_, f32[32,512]{1,0:T(8,128)S(1)} %collective-permute-done.1.refs_2_, bf16[4,64,512]{2,1,0:T(8,128)(2,1)S(1)} %get-tuple-element.16.refs_3_, ...), custom_call_target="tpu_custom_call" | custom-call | tf_op jit(solution)/shard_map/other_side/pallas_call | solution.py:19
  8.9 1.6 %collective-permute-start.3 = (f32[264,128]{1,0:T(8,128)S(1)}, f32[264,128]{1,0:T(8,128)S(1)}, u32[]{:S(2)}, u32[]{:S(2)}) collective-permute-start(f32[264,128]{1,0:T(8,128)S(1)} %get-tuple-element.22), channel_id=1, source_target_pairs={{0,4},{4,0},{8,12},{12,8},{16,20},{20,16},{24,28},{28,24},{1,5},{5... | collective-permute-start | bytes 405512 | tf_op jit(solution)/shard_map/ppermute | solution.py:231
  10.5 4.5 %own_side.1.own_ref = f32[4,64,128]{2,1,0:T(8,128)S(1)} custom-call(bf16[4,64,512]{2,1,0:T(8,128)(2,1)S(1)} %get-tuple-element.20.w_split, f32[2048,2048]{1,0:T(8,128)} %data_ref.1), custom_call_target="tpu_custom_call" | custom-call | tf_op jit(solution)/shard_map/own_side/pallas_call | solution.py:19
  15.0 0.0 collective-permute-done.3.refs_0_
  15.0 2.7 %collective-permute-start.4 = (f32[72,128]{1,0:T(8,128)S(1)}, f32[72,128]{1,0:T(8,128)S(1)}, u32[]{:S(2)}, u32[]{:S(2)}) collective-permute-start(f32[72,128]{1,0:T(8,128)S(1)} %get-tuple-element.23), channel_id=1, source_target_pairs={{0,16},{4,20},{8,24},{12,28},{16,0},{20,4},{24,8},{28,12},{1,17},{... | collective-permute-start | bytes 110600 | tf_op jit(solution)/shard_map/ppermute | solution.py:231
  17.7 1.4 %collective-permute-start.5 = (f32[72,128]{1,0:T(8,128)S(1)}, f32[72,128]{1,0:T(8,128)S(1)}, u32[]{:S(2)}, u32[]{:S(2)}) collective-permute-start(f32[72,128]{1,0:T(8,128)S(1)} %get-tuple-element.24), channel_id=1, source_target_pairs={{0,24},{4,28},{8,16},{12,20},{16,8},{20,12},{24,0},{28,4},{1,25},{... | collective-permute-start | bytes 110600 | tf_op jit(solution)/shard_map/ppermute | solution.py:231
  19.0 0.2 collective-permute-start.6
  19.2 0.7 %collective-permute-done.4.refs_0_ = f32[72,128]{1,0:T(8,128)S(1)} collective-permute-done((f32[72,128]{1,0:T(8,128)S(1)}, f32[72,128]{1,0:T(8,128)S(1)}, u32[]{:S(2)}, u32[]{:S(2)}) %collective-permute-start.4) | collective-permute-done | bytes 36896 | tf_op jit(solution)/shard_map/ppermute | solution.py:231
  19.9 3.5 %collective-permute-done.5.refs_1_ = f32[72,128]{1,0:T(8,128)S(1)} collective-permute-done((f32[72,128]{1,0:T(8,128)S(1)}, f32[72,128]{1,0:T(8,128)S(1)}, u32[]{:S(2)}, u32[]{:S(2)}) %collective-permute-start.5) | collective-permute-done | bytes 36896 | tf_op jit(solution)/shard_map/ppermute | solution.py:231
  23.4 0.0 collective-permute-done.6.refs_2_
  23.4 0.0 copy-done
  23.4 0.5 %row_sweep.1 = f32[8,32,256]{2,1,0:T(8,128)S(1)} custom-call(f32[72,128]{1,0:T(8,128)S(1)} %collective-permute-done.4.refs_0_, f32[72,128]{1,0:T(8,128)S(1)} %collective-permute-done.5.refs_1_, f32[72,128]{1,0:T(8,128)S(1)} %collective-permute-done.6.refs_2_, f32[72,128]{1,0:T(8,128)S(1)} %get-tuple-element.26.refs_3_, f32[32,2048]{1,0:T(8,128)S(1)} %copy-done), custom_call_target="tpu_custom_call" | custom-call | tf_op jit(solution)/shard_map/row_sweep/pallas_call | solution.py:19
  23.9 11.3 %all_to_all.5.pieces = f32[8,32,256]{2,1,0:T(8,128)S(1)} all-to-all(f32[8,32,256]{2,1,0:T(8,128)S(1)} %row_sweep.1), channel_id=1, replica_groups=mesh['prow'=8,'pcol'=4] {'prow'}, dimensions={0} | all-to-all | bytes 524288 | tf_op jit(solution)/shard_map/all_to_all | solution.py:280
  35.2 0.8 %assemble.1 = f32[32,2048]{1,0:T(8,128)} custom-call(f32[8,32,256]{2,1,0:T(8,128)S(1)} %all_to_all.5.pieces), custom_call_target="tpu_custom_call" | custom-call | tf_op jit(solution)/shard_map/assemble/pallas_call | solution.py:19
  (1 shorter events, 0.0 us)
Async XLA Ops:
  0.0 7.5 %copy-start.1 = (f32[32,512]{1,0:T(8,128)S(1)}, f32[32,512]{1,0:T(8,128)}, u32[]{:S(2)}) copy-start(f32[32,512]{1,0:T(8,128)} %refs_0_.1) | copy-start | bytes 196612
  0.0 3.1 %collective-permute-start.2 = (f32[32,512]{1,0:T(8,128)}, f32[32,512]{1,0:T(8,128)S(1)}, u32[]{:S(2)}, u32[]{:S(2)}) collective-permute-start(f32[32,512]{1,0:T(8,128)} %refs_0_.1), channel_id=1, source_target_pairs={{0,1},{1,0},{2,3},{3,2},{4,5},{5,4},{6,7},{7,6},{8,9},{9,8},{10,11... | collective-permute-start | bytes 196616 | tf_op jit(solution)/shard_map/ppermute | solution.py:231
  0.5 6.4 %collective-permute-start.1 = (f32[32,512]{1,0:T(8,128)}, f32[32,512]{1,0:T(8,128)S(1)}, u32[]{:S(2)}, u32[]{:S(2)}) collective-permute-start(f32[32,512]{1,0:T(8,128)} %refs_0_.1), channel_id=1, source_target_pairs={{0,3},{1,2},{2,1},{3,0},{4,7},{5,6},{6,5},{7,4},{8,11},{9,10},{10,... | collective-permute-start | bytes 196616 | tf_op jit(solution)/shard_map/ppermute | solution.py:231
  3.1 4.5 %collective-permute-start = (f32[32,512]{1,0:T(8,128)}, f32[32,512]{1,0:T(8,128)S(1)}, u32[]{:S(2)}, u32[]{:S(2)}) collective-permute-start(f32[32,512]{1,0:T(8,128)} %refs_0_.1), channel_id=1, source_target_pairs={{0,2},{1,3},{2,0},{3,1},{4,6},{5,7},{6,4},{7,5},{8,10},{9,11},{10,... | collective-permute-start | bytes 196616 | tf_op jit(solution)/shard_map/ppermute | solution.py:231
  6.8 16.6 %copy-start = (f32[32,2048]{1,0:T(8,128)S(1)}, f32[32,2048]{1,0:T(8,128)}, u32[]{:S(2)}) copy-start(f32[32,2048]{1,0:T(8,128)} %refs_4_.1) | copy-start | bytes 786436
  8.9 6.0 %collective-permute-start.3 = (f32[264,128]{1,0:T(8,128)S(1)}, f32[264,128]{1,0:T(8,128)S(1)}, u32[]{:S(2)}, u32[]{:S(2)}) collective-permute-start(f32[264,128]{1,0:T(8,128)S(1)} %get-tuple-element.22), channel_id=1, source_target_pairs={{0,4},{4,0},{8,12},{12,8},{16,20},{20,16},{24,28},{28,24},{1,5},{5... | collective-permute-start | bytes 405512 | tf_op jit(solution)/shard_map/ppermute | solution.py:231
  15.0 4.9 %collective-permute-start.4 = (f32[72,128]{1,0:T(8,128)S(1)}, f32[72,128]{1,0:T(8,128)S(1)}, u32[]{:S(2)}, u32[]{:S(2)}) collective-permute-start(f32[72,128]{1,0:T(8,128)S(1)} %get-tuple-element.23), channel_id=1, source_target_pairs={{0,16},{4,20},{8,24},{12,28},{16,0},{20,4},{24,8},{28,12},{1,17},{... | collective-permute-start | bytes 110600 | tf_op jit(solution)/shard_map/ppermute | solution.py:231
  17.7 5.8 %collective-permute-start.5 = (f32[72,128]{1,0:T(8,128)S(1)}, f32[72,128]{1,0:T(8,128)S(1)}, u32[]{:S(2)}, u32[]{:S(2)}) collective-permute-start(f32[72,128]{1,0:T(8,128)S(1)} %get-tuple-element.24), channel_id=1, source_target_pairs={{0,24},{4,28},{8,16},{12,20},{16,8},{20,12},{24,0},{28,4},{1,25},{... | collective-permute-start | bytes 110600 | tf_op jit(solution)/shard_map/ppermute | solution.py:231
  19.0 4.4 %collective-permute-start.6 = (f32[72,128]{1,0:T(8,128)S(1)}, f32[72,128]{1,0:T(8,128)S(1)}, u32[]{:S(2)}, u32[]{:S(2)}) collective-permute-start(f32[72,128]{1,0:T(8,128)S(1)} %get-tuple-element.25), channel_id=1, source_target_pairs={{0,8},{4,12},{8,0},{12,4},{16,24},{20,28},{24,16},{28,20},{1,9},{5... | collective-permute-start | bytes 110600 | tf_op jit(solution)/shard_map/ppermute | solution.py:231
where the time goes:
time: 36.1 us; the launch traced here: 36 us
  blocking collectives  11.3 us (31%)
  Pallas kernels  10.8 us (30%)
  starting transfers between devices  8.92 us (25%)
  waiting for transfers between devices  4.86 us (13%)
    all_to_all x1, blocking collectives, shards(): pieces = lax.all_to_all(fresh, 'prow', 0, 0)  11.3 us
    pallas_call x6, Pallas kernels, call(): pl.pallas_call(kernel, out_shape=out_shape, in_specs=in_specs or [VMEM] *...  10.8 us
    ppermute x7, starting transfers between devices, permute(): return lax.ppermute(value, axis, [(i, i ^ turn) for i in range(size)])  8.92 us
    ppermute x7, waiting for transfers between devices, permute(): return lax.ppermute(value, axis, [(i, i ^ turn) for i in range(size)])  4.86 us
  transfers between devices with their start and end apart: 7, of which 3 were waited for; matrix products, arithmetic and copies ran while one was open for 0% of the time, Pallas kernels for 23%

commit v1 on v0

--- a/solution.py
+++ b/solution.py
@@ -165,34 +165,48 @@
         own_region(functools.partial(multiply, at))
 
 
-def side_sum_kernel(slab, own_ref, gram_ref, *refs):
-    far = own_ref.shape[0]
-    got_refs, out_refs = refs[:-far], refs[-far:]
+def side_sum_kernel(slab, turns, pairs, own_ref, gram_ref, *refs):
+    got_refs, out_refs = refs[: -len(pairs)], refs[-len(pairs) :]
     gram = gram_ref[...]
     for got in got_refs:
-        gram = gram + got[slab * far :]
-    for at, out_ref in enumerate(out_refs):
-        total = own_ref[at]
-        for got in got_refs:
-            total = total + got[slab * at : slab * (at + 1)]
-        out_ref[:slab] = total
-        out_ref[slab:] = gram
-
-
-def sweep_kernel(width, *refs):
+        gram = gram + got[slab * len(turns) :]
+    for pair, out_ref in zip(pairs, out_refs):
+        for at, turn in enumerate(pair):
+            place = turns.index(turn)
+            total = own_ref[place]
+            for got in got_refs:
+                total = total + got[slab * place : slab * (place + 1)]
+            out_ref[slab * at : slab * (at + 1)] = total
+        out_ref[slab * len(pair) :] = gram
+
+
+def peer_start(near, width, level, side):
+    return pl.multiple_of((level * near + side) * width, width)
+
+
+def sweep_kernel(near, width, swapped, *refs):
     parts, h_ref, out_ref = refs[:-2], refs[-2], refs[-1]
     rank = h_ref.shape[0]
     row_at = lax.axis_index("prow")
-    total = parts[0][...]
-    for part in parts[1:]:
-        total = total + part[...]
+    side, level = lax.rem(row_at, near), lax.div(row_at, near)
     pieces = width // LANES
-    cross = jnp.concatenate([total[rank * i : rank * (i + 1)] for i in range(pieces)], axis=1)
-    packed = total[rank * pieces :]
+    slab = rank * pieces
+    packed, chunks = None, [None, None]
+    for part, swap in zip(parts, swapped):
+        gram_part = part[2 * slab :]
+        packed = gram_part if packed is None else packed + gram_part
+        for at in range(2):
+            place = 1 - at if swap else at
+            piece = part[slab * place : slab * (place + 1)]
+            chunks[at] = piece if chunks[at] is None else chunks[at] + piece
+    cross = jnp.concatenate(
+        [chunk[rank * i : rank * (i + 1)] for chunk in chunks for i in range(pieces)], axis=1
+    )
     gram = jnp.concatenate(
         [packed[:, rank * i : rank * (i + 1)] for i in range(rank // GRAM_ROWS)], axis=0
     )
-    h = h_ref[:, pl.ds(pl.multiple_of(row_at * width, width), width)]
+    starts = [peer_start(near, width, at, side) for at in (level, level ^ 2)]
+    h = jnp.concatenate([h_ref[:, pl.ds(start, width)] for start in starts], axis=1)
     rest = cross - exact_dot(gram, h, ((1,), (0,)))
     rows = []
     for k in range(rank):
@@ -202,16 +216,24 @@
         rows.append(fresh)
         rest = rest - gram[:, k : k + 1] * (fresh - old)
     done = jnp.concatenate(rows, axis=0)
-    for peer in range(out_ref.shape[0]):
-        out_ref[peer] = done
-
-
-def assemble_kernel(width, pieces, out_ref, sems):
+    for member in range(out_ref.shape[0]):
+        for at in range(2):
+            out_ref[member, at] = done[:, width * at : width * (at + 1)]
+
+
+def assemble_kernel(near, width, pieces, out_ref, sems):
+    level = lax.div(lax.axis_index("prow"), near)
     copies = []
-    for peer in range(pieces.shape[0]):
-        columns = pl.ds(width * peer, width)
-        copies.append(pltpu.make_async_copy(pieces.at[peer], out_ref.at[:, columns], sems.at[peer]))
-        copies[-1].start()
+    for member in range(pieces.shape[0]):
+        above, side = member // near, member % near
+        theirs = lax.div(level, 2) * 2 + above
+        for at, source in enumerate((theirs, theirs ^ 2)):
+            columns = pl.ds(peer_start(near, width, source, side), width)
+            copy = pltpu.make_async_copy(
+                pieces.at[member, at], out_ref.at[:, columns], sems.at[member, at]
+            )
+            copy.start()
+            copies.append(copy)
     for copy in copies:
         copy.wait()
 
@@ -265,22 +287,23 @@
             pltpu.SemaphoreType.DMA((far, n_col)),
         ],
     )
+    pairs = [(2, 0), (3, 1), (1, 3)]
     sums = call(
-        functools.partial(side_sum_kernel, slab),
-        [floats(slab + GRAM_ROWS, LANES)] * far, [own, gram, *got], "side_sum",
-    )
-    parts = [
-        permute(value, "prow", turn * near) if turn else value
-        for turn, value in zip(turns, sums)
-    ]
+        functools.partial(side_sum_kernel, slab, turns, pairs),
+        [floats(2 * slab + GRAM_ROWS, LANES)] * len(pairs), [own, gram, *got], "side_sum",
+    )
+    parts = [permute(value, "prow", pair[0] * near) for pair, value in zip(pairs, sums)]
+    parts.append(sums[0])
+    members = 2 * near
     fresh = call(
-        functools.partial(sweep_kernel, width), floats(n_row, rank, width),
-        [*parts, h_prior], "row_sweep",
-    )
-    pieces = lax.all_to_all(fresh, "prow", 0, 0)
+        functools.partial(sweep_kernel, near, width, [False, False, False, True]),
+        floats(members, 2, rank, width), [*parts, h_prior], "row_sweep",
+    )
+    groups = [[low + at for at in range(members)] for low in range(0, n_row, members)]
+    pieces = lax.all_to_all(fresh, "prow", 0, 0, axis_index_groups=groups)
     return call(
-        functools.partial(assemble_kernel, width), floats(rank, cols), [pieces], "assemble",
-        scratch=[pltpu.SemaphoreType.DMA((n_row,))], out_specs=HBM,
+        functools.partial(assemble_kernel, near, width), floats(rank, cols), [pieces],
+        "assemble", scratch=[pltpu.SemaphoreType.DMA((members, 2))], out_specs=HBM,
     )
 
 

time: 36.1 us -> 34.1 us (0.945)
  blocking collectives: 11.3 us -> 8.73 us
    all_to_all x1, blocking collectives: 11.3 us -> 8.73 us  [shards(): pieces = lax.all_to_all(fresh, 'prow', 0, 0, axis_index_groups=groups)]
  transfers between devices with their start and end apart: 7 -> 7, of which waited for: 3 -> 4; matrix products, arithmetic and copies ran while one was open for 0% -> 0% of each run, Pallas kernels for 23% -> 24%
where the time goes in v1:
time: 34.1 us; the launch traced here: 34 us
  Pallas kernels  10.8 us (32%)
  starting transfers between devices  9.14 us (27%)
  blocking collectives  8.73 us (26%)
  waiting for transfers between devices  5.19 us (15%)
    pallas_call x6, Pallas kernels, call(): pl.pallas_call(kernel, out_shape=out_shape, in_specs=in_specs or [VMEM] *...  10.8 us
    ppermute x7, starting transfers between devices, permute(): return lax.ppermute(value, axis, [(i, i ^ turn) for i in range(size)])  9.14 us
    all_to_all x1, blocking collectives, shards(): pieces = lax.all_to_all(fresh, 'prow', 0, 0, axis_index_groups=groups)  8.73 us
    ppermute x7, waiting for transfers between devices, permute(): return lax.ppermute(value, axis, [(i, i ^ turn) for i in range(size)])  5.19 us
  transfers between devices with their start and end apart: 7, of which 4 were waited for; matrix products, arithmetic and copies ran while one was open for 0% of the time, Pallas kernels for 24%

profile of v1, /device:TPU:0, one launch (start us, length us, event | category | flops | bytes accessed | tf_op | source)
XLA Modules:
  0.0 34.0 jit_solution(17354392128957261218)
XLA Ops:
  0.0 0.0 copy-start.1
  0.0 0.5 %collective-permute-start.2 = (f32[32,512]{1,0:T(8,128)}, f32[32,512]{1,0:T(8,128)S(1)}, u32[]{:S(2)}, u32[]{:S(2)}) collective-permute-start(f32[32,512]{1,0:T(8,128)} %refs_0_.1), channel_id=1, source_target_pairs={{0,1},{1,0},{2,3},{3,2},{4,5},{5,4},{6,7},{7,6},{8,9},{9,8},{10,11... | collective-permute-start | bytes 196616 | tf_op jit(solution)/shard_map/ppermute | solution.py:253
  0.5 2.6 %collective-permute-start.1 = (f32[32,512]{1,0:T(8,128)}, f32[32,512]{1,0:T(8,128)S(1)}, u32[]{:S(2)}, u32[]{:S(2)}) collective-permute-start(f32[32,512]{1,0:T(8,128)} %refs_0_.1), channel_id=1, source_target_pairs={{0,3},{1,2},{2,1},{3,0},{4,7},{5,6},{6,5},{7,4},{8,11},{9,10},{10,... | collective-permute-start | bytes 196616 | tf_op jit(solution)/shard_map/ppermute | solution.py:253
  3.1 0.1 collective-permute-start
  3.1 0.0 collective-permute-done.2.refs_0_
  3.1 3.7 %load_other_side.1 = (f32[4,2048,256]{2,1,0:T(8,128)S(1)}, f32[4,64,128]{2,1,0:T(8,128)S(1)}, bf16[4,64,512]{2,1,0:T(8,128)(2,1)S(1)}, f32[32,32]{1,0:T(8,128)S(1)}) custom-call(f32[32,512]{1,0:T(8,128)S(1)} %collective-permute-done.2.refs_0_, f32[2048,2048]{1,0:T(8,128)} %data_ref.1), custom_call_target="tpu_custom_call" | custom-call | bytes 16777216 | tf_op jit(solution)/shard_map/load_other_side/pallas_call | solution.py:19
  6.8 0.0 copy-start
  6.8 0.0 collective-permute-done.1.refs_2_
  6.9 0.7 %collective-permute-done.refs_1_ = f32[32,512]{1,0:T(8,128)S(1)} collective-permute-done((f32[32,512]{1,0:T(8,128)}, f32[32,512]{1,0:T(8,128)S(1)}, u32[]{:S(2)}, u32[]{:S(2)}) %collective-permute-start) | collective-permute-done | bytes 65568 | tf_op jit(solution)/shard_map/ppermute | solution.py:253
  7.5 0.0 copy-done.1
  7.5 1.4 %other_side.1 = (f32[264,128]{1,0:T(8,128)S(1)}, bf16[4,64,512]{2,1,0:T(8,128)(2,1)S(1)}, f32[8,128]{1,0:T(8,128)S(1)}) custom-call(f32[32,512]{1,0:T(8,128)S(1)} %copy-done.1, f32[32,512]{1,0:T(8,128)S(1)} %collective-permute-done.refs_1_, f32[32,512]{1,0:T(8,128)S(1)} %collective-permute-done.1.refs_2_, bf16[4,64,512]{2,1,0:T(8,128)(2,1)S(1)} %get-tuple-element.15.refs_3_, ...), custom_call_target="tpu_custom_call" | custom-call | tf_op jit(solution)/shard_map/other_side/pallas_call | solution.py:19
  8.9 1.6 %collective-permute-start.3 = (f32[264,128]{1,0:T(8,128)S(1)}, f32[264,128]{1,0:T(8,128)S(1)}, u32[]{:S(2)}, u32[]{:S(2)}) collective-permute-start(f32[264,128]{1,0:T(8,128)S(1)} %get-tuple-element.21), channel_id=1, source_target_pairs={{0,4},{4,0},{8,12},{12,8},{16,20},{20,16},{24,28},{28,24},{1,5},{5... | collective-permute-start | bytes 405512 | tf_op jit(solution)/shard_map/ppermute | solution.py:253
  10.5 4.5 %own_side.1.own_ref = f32[4,64,128]{2,1,0:T(8,128)S(1)} custom-call(bf16[4,64,512]{2,1,0:T(8,128)(2,1)S(1)} %get-tuple-element.19.w_split, f32[2048,2048]{1,0:T(8,128)} %data_ref.1), custom_call_target="tpu_custom_call" | custom-call | tf_op jit(solution)/shard_map/own_side/pallas_call | solution.py:19
  15.0 0.0 collective-permute-done.3.refs_0_
  15.0 3.7 %collective-permute-start.5 = (f32[136,128]{1,0:T(8,128)S(1)}, f32[136,128]{1,0:T(8,128)S(1)}, u32[]{:S(2)}, u32[]{:S(2)}) collective-permute-start(f32[136,128]{1,0:T(8,128)S(1)} %get-tuple-element.23), channel_id=1, source_target_pairs={{0,24},{4,28},{8,16},{12,20},{16,8},{20,12},{24,0},{28,4},{1,25},{... | collective-permute-start | bytes 208904 | tf_op jit(solution)/shard_map/ppermute | solution.py:253
  18.7 0.0 collective-permute-start.6
  18.7 0.8 %collective-permute-start.4 = (f32[136,128]{1,0:T(8,128)S(1)}, f32[136,128]{1,0:T(8,128)S(1)}, u32[]{:S(2)}, u32[]{:S(2)}) collective-permute-start(f32[136,128]{1,0:T(8,128)S(1)} %get-tuple-element.22.refs_3_), channel_id=1, source_target_pairs={{0,16},{4,20},{8,24},{12,28},{16,0},{20,4},{24,8},{28,12},{1,17},{... | collective-permute-start | bytes 208904 | tf_op jit(solution)/shard_map/ppermute | solution.py:253
  19.5 1.8 %collective-permute-done.5.refs_1_ = f32[136,128]{1,0:T(8,128)S(1)} collective-permute-done((f32[136,128]{1,0:T(8,128)S(1)}, f32[136,128]{1,0:T(8,128)S(1)}, u32[]{:S(2)}, u32[]{:S(2)}) %collective-permute-start.5) | collective-permute-done | bytes 69664 | tf_op jit(solution)/shard_map/ppermute | solution.py:253
  21.3 2.0 %collective-permute-done.6.refs_2_ = f32[136,128]{1,0:T(8,128)S(1)} collective-permute-done((f32[136,128]{1,0:T(8,128)S(1)}, f32[136,128]{1,0:T(8,128)S(1)}, u32[]{:S(2)}, u32[]{:S(2)}) %collective-permute-start.6) | collective-permute-done | bytes 69664 | tf_op jit(solution)/shard_map/ppermute | solution.py:253
  23.2 0.7 %collective-permute-done.4.refs_0_ = f32[136,128]{1,0:T(8,128)S(1)} collective-permute-done((f32[136,128]{1,0:T(8,128)S(1)}, f32[136,128]{1,0:T(8,128)S(1)}, u32[]{:S(2)}, u32[]{:S(2)}) %collective-permute-start.4) | collective-permute-done | bytes 69664 | tf_op jit(solution)/shard_map/ppermute | solution.py:253
  24.0 0.0 copy-done
  24.0 0.5 %row_sweep.1 = f32[4,2,32,256]{3,2,1,0:T(8,128)S(1)} custom-call(f32[136,128]{1,0:T(8,128)S(1)} %collective-permute-done.4.refs_0_, f32[136,128]{1,0:T(8,128)S(1)} %collective-permute-done.5.refs_1_, f32[136,128]{1,0:T(8,128)S(1)} %collective-permute-done.6.refs_2_, f32[136,128]{1,0:T(8,128)S(1)} %get-tuple-element.22.refs_3_, f32[32,2048]{1,0:T(8,128)S(1)} %copy-done), custom_call_target="tpu_custom_call" | custom-call | tf_op jit(solution)/shard_map/row_sweep/pallas_call | solution.py:19
  24.5 8.7 %all_to_all.5.pieces = f32[4,2,32,256]{3,2,1,0:T(8,128)S(1)} all-to-all(f32[4,2,32,256]{3,2,1,0:T(8,128)S(1)} %row_sweep.1), channel_id=1, replica_groups={{0,4,8,12},{16,20,24,28},{1,5,9,13},{17,21,25,29},{2,6,10,14},{18,22,26..., dimensions={0} | all-to-all | bytes 524288 | tf_op jit(solution)/shard_map/all_to_all | solution.py:303
  33.2 0.8 %assemble.1 = f32[32,2048]{1,0:T(8,128)} custom-call(f32[4,2,32,256]{3,2,1,0:T(8,128)S(1)} %all_to_all.5.pieces), custom_call_target="tpu_custom_call" | custom-call | tf_op jit(solution)/shard_map/assemble/pallas_call | solution.py:19
  (1 shorter events, 0.0 us)
Async XLA Ops:
  0.0 7.5 %copy-start.1 = (f32[32,512]{1,0:T(8,128)S(1)}, f32[32,512]{1,0:T(8,128)}, u32[]{:S(2)}) copy-start(f32[32,512]{1,0:T(8,128)} %refs_0_.1) | copy-start | bytes 196612
  0.0 3.1 %collective-permute-start.2 = (f32[32,512]{1,0:T(8,128)}, f32[32,512]{1,0:T(8,128)S(1)}, u32[]{:S(2)}, u32[]{:S(2)}) collective-permute-start(f32[32,512]{1,0:T(8,128)} %refs_0_.1), channel_id=1, source_target_pairs={{0,1},{1,0},{2,3},{3,2},{4,5},{5,4},{6,7},{7,6},{8,9},{9,8},{10,11... | collective-permute-start | bytes 196616 | tf_op jit(solution)/shard_map/ppermute | solution.py:253
  0.5 6.4 %collective-permute-start.1 = (f32[32,512]{1,0:T(8,128)}, f32[32,512]{1,0:T(8,128)S(1)}, u32[]{:S(2)}, u32[]{:S(2)}) collective-permute-start(f32[32,512]{1,0:T(8,128)} %refs_0_.1), channel_id=1, source_target_pairs={{0,3},{1,2},{2,1},{3,0},{4,7},{5,6},{6,5},{7,4},{8,11},{9,10},{10,... | collective-permute-start | bytes 196616 | tf_op jit(solution)/shard_map/ppermute | solution.py:253
  3.1 4.5 %collective-permute-start = (f32[32,512]{1,0:T(8,128)}, f32[32,512]{1,0:T(8,128)S(1)}, u32[]{:S(2)}, u32[]{:S(2)}) collective-permute-start(f32[32,512]{1,0:T(8,128)} %refs_0_.1), channel_id=1, source_target_pairs={{0,2},{1,3},{2,0},{3,1},{4,6},{5,7},{6,4},{7,5},{8,10},{9,11},{10,... | collective-permute-start | bytes 196616 | tf_op jit(solution)/shard_map/ppermute | solution.py:253
  6.8 17.1 %copy-start = (f32[32,2048]{1,0:T(8,128)S(1)}, f32[32,2048]{1,0:T(8,128)}, u32[]{:S(2)}) copy-start(f32[32,2048]{1,0:T(8,128)} %refs_4_.1) | copy-start | bytes 786436
  8.9 6.0 %collective-permute-start.3 = (f32[264,128]{1,0:T(8,128)S(1)}, f32[264,128]{1,0:T(8,128)S(1)}, u32[]{:S(2)}, u32[]{:S(2)}) collective-permute-start(f32[264,128]{1,0:T(8,128)S(1)} %get-tuple-element.21), channel_id=1, source_target_pairs={{0,4},{4,0},{8,12},{12,8},{16,20},{20,16},{24,28},{28,24},{1,5},{5... | collective-permute-start | bytes 405512 | tf_op jit(solution)/shard_map/ppermute | solution.py:253
  15.0 6.3 %collective-permute-start.5 = (f32[136,128]{1,0:T(8,128)S(1)}, f32[136,128]{1,0:T(8,128)S(1)}, u32[]{:S(2)}, u32[]{:S(2)}) collective-permute-start(f32[136,128]{1,0:T(8,128)S(1)} %get-tuple-element.23), channel_id=1, source_target_pairs={{0,24},{4,28},{8,16},{12,20},{16,8},{20,12},{24,0},{28,4},{1,25},{... | collective-permute-start | bytes 208904 | tf_op jit(solution)/shard_map/ppermute | solution.py:253
  18.7 4.6 %collective-permute-start.6 = (f32[136,128]{1,0:T(8,128)S(1)}, f32[136,128]{1,0:T(8,128)S(1)}, u32[]{:S(2)}, u32[]{:S(2)}) collective-permute-start(f32[136,128]{1,0:T(8,128)S(1)} %get-tuple-element.24), channel_id=1, source_target_pairs={{0,8},{4,12},{8,0},{12,4},{16,24},{20,28},{24,16},{28,20},{1,9},{5... | collective-permute-start | bytes 208904 | tf_op jit(solution)/shard_map/ppermute | solution.py:253
  18.7 5.3 %collective-permute-start.4 = (f32[136,128]{1,0:T(8,128)S(1)}, f32[136,128]{1,0:T(8,128)S(1)}, u32[]{:S(2)}, u32[]{:S(2)}) collective-permute-start(f32[136,128]{1,0:T(8,128)S(1)} %get-tuple-element.22.refs_3_), channel_id=1, source_target_pairs={{0,16},{4,20},{8,24},{12,28},{16,0},{20,4},{24,8},{28,12},{1,17},{... | collective-permute-start | bytes 208904 | tf_op jit(solution)/shard_map/ppermute | solution.py:253

commit v2 on v1

--- a/solution.py
+++ b/solution.py
@@ -184,7 +184,7 @@
     return pl.multiple_of((level * near + side) * width, width)
 
 
-def sweep_kernel(near, width, swapped, *refs):
+def sweep_kernel(near, width, *refs):
     parts, h_ref, out_ref = refs[:-2], refs[-2], refs[-1]
     rank = h_ref.shape[0]
     row_at = lax.axis_index("prow")
@@ -192,12 +192,11 @@
     pieces = width // LANES
     slab = rank * pieces
     packed, chunks = None, [None, None]
-    for part, swap in zip(parts, swapped):
+    for part in parts:
         gram_part = part[2 * slab :]
         packed = gram_part if packed is None else packed + gram_part
         for at in range(2):
-            place = 1 - at if swap else at
-            piece = part[slab * place : slab * (place + 1)]
+            piece = part[slab * at : slab * (at + 1)]
             chunks[at] = piece if chunks[at] is None else chunks[at] + piece
     cross = jnp.concatenate(
         [chunk[rank * i : rank * (i + 1)] for chunk in chunks for i in range(pieces)], axis=1
@@ -216,21 +215,21 @@
         rows.append(fresh)
         rest = rest - gram[:, k : k + 1] * (fresh - old)
     done = jnp.concatenate(rows, axis=0)
-    for member in range(out_ref.shape[0]):
-        for at in range(2):
-            out_ref[member, at] = done[:, width * at : width * (at + 1)]
-
-
-def assemble_kernel(near, width, pieces, out_ref, sems):
-    level = lax.div(lax.axis_index("prow"), near)
+    for at in range(2):
+        out_ref[at] = done[:, width * at : width * (at + 1)]
+
+
+def assemble_kernel(near, width, members, *refs):
+    piece_refs, (out_ref, sems) = refs[:-2], refs[-2:]
+    row_at = lax.axis_index("prow")
+    side, level = lax.rem(row_at, near), lax.div(row_at, near)
     copies = []
-    for member in range(pieces.shape[0]):
-        above, side = member // near, member % near
-        theirs = lax.div(level, 2) * 2 + above
+    for member, ((above, side_turn), piece_ref) in enumerate(zip(members, piece_refs)):
+        theirs = level ^ above
         for at, source in enumerate((theirs, theirs ^ 2)):
-            columns = pl.ds(peer_start(near, width, source, side), width)
+            columns = pl.ds(peer_start(near, width, source, side ^ side_turn), width)
             copy = pltpu.make_async_copy(
-                pieces.at[member, at], out_ref.at[:, columns], sems.at[member, at]
+                piece_ref.at[at], out_ref.at[:, columns], sems.at[member, at]
             )
             copy.start()
             copies.append(copy)
@@ -287,23 +286,27 @@
             pltpu.SemaphoreType.DMA((far, n_col)),
         ],
     )
-    pairs = [(2, 0), (3, 1), (1, 3)]
+    pairs = [(2, 0), (3, 1), (1, 3), (0, 2)]
     sums = call(
         functools.partial(side_sum_kernel, slab, turns, pairs),
         [floats(2 * slab + GRAM_ROWS, LANES)] * len(pairs), [own, gram, *got], "side_sum",
     )
-    parts = [permute(value, "prow", pair[0] * near) for pair, value in zip(pairs, sums)]
-    parts.append(sums[0])
-    members = 2 * near
+    parts = [
+        permute(value, "prow", pair[0] * near) if pair[0] else value
+        for pair, value in zip(pairs, sums)
+    ]
     fresh = call(
-        functools.partial(sweep_kernel, near, width, [False, False, False, True]),
-        floats(members, 2, rank, width), [*parts, h_prior], "row_sweep",
-    )
-    groups = [[low + at for at in range(members)] for low in range(0, n_row, members)]
-    pieces = lax.all_to_all(fresh, "prow", 0, 0, axis_index_groups=groups)
+        functools.partial(sweep_kernel, near, width), floats(2, rank, width), [*parts, h_prior],
+        "row_sweep",
+    )
+    members = [(above, side) for above in range(2) for side in range(near)]
+    pieces = [
+        permute(fresh, "prow", above * near + side) if above or side else fresh
+        for above, side in members
+    ]
     return call(
-        functools.partial(assemble_kernel, near, width), floats(rank, cols), [pieces],
-        "assemble", scratch=[pltpu.SemaphoreType.DMA((members, 2))], out_specs=HBM,
+        functools.partial(assemble_kernel, near, width, members), floats(rank, cols), pieces,
+        "assemble", scratch=[pltpu.SemaphoreType.DMA((len(members), 2))], out_specs=HBM,
     )
 
 

time: 34.1 us -> 31.8 us (0.933)
  blocking collectives: 8.73 us -> 0 us
  starting transfers between devices: 9.14 us -> 12.5 us
  waiting for transfers between devices: 5.19 us -> 8.3 us
    all_to_all x1 -> x0, blocking collectives: 8.73 us -> none  [shards(): pieces = lax.all_to_all(fresh, 'prow', 0, 0, axis_index_groups=groups)]
    ppermute x7 -> x10, starting transfers between devices: 9.14 us -> 12.5 us  [permute(): return lax.ppermute(value, axis, [(i, i ^ turn) for i in range(size)])]
    ppermute x7 -> x10, waiting for transfers between devices: 5.19 us -> 8.3 us  [permute(): return lax.ppermute(value, axis, [(i, i ^ turn) for i in range(size)])]
  transfers between devices with their start and end apart: 7 -> 10, of which waited for: 4 -> 6; matrix products, arithmetic and copies ran while one was open for 0% -> 0% of each run, Pallas kernels for 24% -> 26%
where the time goes in v2:
time: 31.8 us; the launch traced here: 31.7 us
  starting transfers between devices  12.5 us (39%)
  Pallas kernels  10.8 us (34%)
  waiting for transfers between devices  8.3 us (26%)
    ppermute x10, starting transfers between devices, permute(): return lax.ppermute(value, axis, [(i, i ^ turn) for i in range(size)])  12.5 us
    pallas_call x6, Pallas kernels, call(): pl.pallas_call(kernel, out_shape=out_shape, in_specs=in_specs or [VMEM] *...  10.8 us
    ppermute x10, waiting for transfers between devices, permute(): return lax.ppermute(value, axis, [(i, i ^ turn) for i in range(size)])  8.3 us
  transfers between devices with their start and end apart: 10, of which 6 were waited for; matrix products, arithmetic and copies ran while one was open for 0% of the time, Pallas kernels for 26%

profile of v2, /device:TPU:0, one launch (start us, length us, event | category | flops | bytes accessed | tf_op | source)
XLA Modules:
  0.0 31.7 jit_solution(13842258077295525616)
XLA Ops:
  0.0 0.0 copy-start.1
  0.0 0.5 %collective-permute-start.2 = (f32[32,512]{1,0:T(8,128)}, f32[32,512]{1,0:T(8,128)S(1)}, u32[]{:S(2)}, u32[]{:S(2)}) collective-permute-start(f32[32,512]{1,0:T(8,128)} %refs_0_.1), channel_id=1, source_target_pairs={{0,1},{1,0},{2,3},{3,2},{4,5},{5,4},{6,7},{7,6},{8,9},{9,8},{10,11... | collective-permute-start | bytes 196616 | tf_op jit(solution)/shard_map/ppermute | solution.py:252
  0.5 2.6 %collective-permute-start.1 = (f32[32,512]{1,0:T(8,128)}, f32[32,512]{1,0:T(8,128)S(1)}, u32[]{:S(2)}, u32[]{:S(2)}) collective-permute-start(f32[32,512]{1,0:T(8,128)} %refs_0_.1), channel_id=1, source_target_pairs={{0,3},{1,2},{2,1},{3,0},{4,7},{5,6},{6,5},{7,4},{8,11},{9,10},{10,... | collective-permute-start | bytes 196616 | tf_op jit(solution)/shard_map/ppermute | solution.py:252
  3.1 0.1 collective-permute-start
  3.1 0.0 collective-permute-done.2.refs_0_
  3.1 3.7 %load_other_side.1 = (f32[4,2048,256]{2,1,0:T(8,128)S(1)}, f32[4,64,128]{2,1,0:T(8,128)S(1)}, bf16[4,64,512]{2,1,0:T(8,128)(2,1)S(1)}, f32[32,32]{1,0:T(8,128)S(1)}) custom-call(f32[32,512]{1,0:T(8,128)S(1)} %collective-permute-done.2.refs_0_, f32[2048,2048]{1,0:T(8,128)} %data_ref.1), custom_call_target="tpu_custom_call" | custom-call | bytes 16777216 | tf_op jit(solution)/shard_map/load_other_side/pallas_call | solution.py:19
  6.8 0.0 copy-start
  6.8 0.0 collective-permute-done.1.refs_2_
  6.9 0.7 %collective-permute-done.refs_1_ = f32[32,512]{1,0:T(8,128)S(1)} collective-permute-done((f32[32,512]{1,0:T(8,128)}, f32[32,512]{1,0:T(8,128)S(1)}, u32[]{:S(2)}, u32[]{:S(2)}) %collective-permute-start) | collective-permute-done | bytes 65568 | tf_op jit(solution)/shard_map/ppermute | solution.py:252
  7.5 0.0 copy-done.1
  7.5 1.4 %other_side.1 = (f32[264,128]{1,0:T(8,128)S(1)}, bf16[4,64,512]{2,1,0:T(8,128)(2,1)S(1)}, f32[8,128]{1,0:T(8,128)S(1)}) custom-call(f32[32,512]{1,0:T(8,128)S(1)} %copy-done.1, f32[32,512]{1,0:T(8,128)S(1)} %collective-permute-done.refs_1_, f32[32,512]{1,0:T(8,128)S(1)} %collective-permute-done.1.refs_2_, bf16[4,64,512]{2,1,0:T(8,128)(2,1)S(1)} %get-tuple-element.16.refs_3_, ...), custom_call_target="tpu_custom_call" | custom-call | tf_op jit(solution)/shard_map/other_side/pallas_call | solution.py:19
  8.9 1.6 %collective-permute-start.3 = (f32[264,128]{1,0:T(8,128)S(1)}, f32[264,128]{1,0:T(8,128)S(1)}, u32[]{:S(2)}, u32[]{:S(2)}) collective-permute-start(f32[264,128]{1,0:T(8,128)S(1)} %get-tuple-element.22), channel_id=1, source_target_pairs={{0,4},{4,0},{8,12},{12,8},{16,20},{20,16},{24,28},{28,24},{1,5},{5... | collective-permute-start | bytes 405512 | tf_op jit(solution)/shard_map/ppermute | solution.py:252
  10.5 4.5 %own_side.1.own_ref = f32[4,64,128]{2,1,0:T(8,128)S(1)} custom-call(bf16[4,64,512]{2,1,0:T(8,128)(2,1)S(1)} %get-tuple-element.20.w_split, f32[2048,2048]{1,0:T(8,128)} %data_ref.1), custom_call_target="tpu_custom_call" | custom-call | tf_op jit(solution)/shard_map/own_side/pallas_call | solution.py:19
  15.0 0.0 collective-permute-done.3.refs_0_
  15.0 2.7 %collective-permute-start.4 = (f32[136,128]{1,0:T(8,128)S(1)}, f32[136,128]{1,0:T(8,128)S(1)}, u32[]{:S(2)}, u32[]{:S(2)}) collective-permute-start(f32[136,128]{1,0:T(8,128)S(1)} %get-tuple-element.23), channel_id=1, source_target_pairs={{0,16},{4,20},{8,24},{12,28},{16,0},{20,4},{24,8},{28,12},{1,17},{... | collective-permute-start | bytes 208904 | tf_op jit(solution)/shard_map/ppermute | solution.py:252
  17.7 1.4 %collective-permute-start.5 = (f32[136,128]{1,0:T(8,128)S(1)}, f32[136,128]{1,0:T(8,128)S(1)}, u32[]{:S(2)}, u32[]{:S(2)}) collective-permute-start(f32[136,128]{1,0:T(8,128)S(1)} %get-tuple-element.24), channel_id=1, source_target_pairs={{0,24},{4,28},{8,16},{12,20},{16,8},{20,12},{24,0},{28,4},{1,25},{... | collective-permute-start | bytes 208904 | tf_op jit(solution)/shard_map/ppermute | solution.py:252
  19.0 0.2 collective-permute-start.6
  19.3 1.2 %collective-permute-done.4.refs_0_ = f32[136,128]{1,0:T(8,128)S(1)} collective-permute-done((f32[136,128]{1,0:T(8,128)S(1)}, f32[136,128]{1,0:T(8,128)S(1)}, u32[]{:S(2)}, u32[]{:S(2)}) %collective-permute-start.4) | collective-permute-done | bytes 69664 | tf_op jit(solution)/shard_map/ppermute | solution.py:252
  20.5 3.5 %collective-permute-done.5.refs_1_ = f32[136,128]{1,0:T(8,128)S(1)} collective-permute-done((f32[136,128]{1,0:T(8,128)S(1)}, f32[136,128]{1,0:T(8,128)S(1)}, u32[]{:S(2)}, u32[]{:S(2)}) %collective-permute-start.5) | collective-permute-done | bytes 69664 | tf_op jit(solution)/shard_map/ppermute | solution.py:252
  23.9 0.1 collective-permute-done.6.refs_2_
  24.1 0.0 copy-done
  24.1 0.5 %row_sweep.1.refs_0_ = f32[2,32,256]{2,1,0:T(8,128)S(1)} custom-call(f32[136,128]{1,0:T(8,128)S(1)} %collective-permute-done.4.refs_0_, f32[136,128]{1,0:T(8,128)S(1)} %collective-permute-done.5.refs_1_, f32[136,128]{1,0:T(8,128)S(1)} %collective-permute-done.6.refs_2_, f32[136,128]{1,0:T(8,128)S(1)} %get-tuple-element.26.refs_3_, f32[32,2048]{1,0:T(8,128)S(1)} %copy-done), custom_call_target="tpu_custom_call" | custom-call | tf_op jit(solution)/shard_map/row_sweep/pallas_call | solution.py:19
  24.6 0.6 %collective-permute-start.9 = (f32[2,32,256]{2,1,0:T(8,128)S(1)}, f32[2,32,256]{2,1,0:T(8,128)S(1)}, u32[]{:S(2)}, u32[]{:S(2)}) collective-permute-start(f32[2,32,256]{2,1,0:T(8,128)S(1)} %row_sweep.1.refs_0_), channel_id=1, source_target_pairs={{0,12},{4,8},{8,4},{12,0},{16,28},{20,24},{24,20},{28,16},{1,13},{... | collective-permute-start | bytes 196616 | tf_op jit(solution)/shard_map/ppermute | solution.py:252
  25.2 1.4 %collective-permute-start.8 = (f32[2,32,256]{2,1,0:T(8,128)S(1)}, f32[2,32,256]{2,1,0:T(8,128)S(1)}, u32[]{:S(2)}, u32[]{:S(2)}) collective-permute-start(f32[2,32,256]{2,1,0:T(8,128)S(1)} %row_sweep.1.refs_0_), channel_id=1, source_target_pairs={{0,8},{4,12},{8,0},{12,4},{16,24},{20,28},{24,16},{28,20},{1,9},{5... | collective-permute-start | bytes 196616 | tf_op jit(solution)/shard_map/ppermute | solution.py:252
  26.7 1.5 %collective-permute-start.7 = (f32[2,32,256]{2,1,0:T(8,128)S(1)}, f32[2,32,256]{2,1,0:T(8,128)S(1)}, u32[]{:S(2)}, u32[]{:S(2)}) collective-permute-start(f32[2,32,256]{2,1,0:T(8,128)S(1)} %row_sweep.1.refs_0_), channel_id=1, source_target_pairs={{0,4},{4,0},{8,12},{12,8},{16,20},{20,16},{24,28},{28,24},{1,5},{5... | collective-permute-start | bytes 196616 | tf_op jit(solution)/shard_map/ppermute | solution.py:252
  28.1 1.7 %collective-permute-done.9.refs_3_ = f32[2,32,256]{2,1,0:T(8,128)S(1)} collective-permute-done((f32[2,32,256]{2,1,0:T(8,128)S(1)}, f32[2,32,256]{2,1,0:T(8,128)S(1)}, u32[]{:S(2)}, u32[]{:S(2)}) %collective-permute-start.9) | collective-permute-done | bytes 65568 | tf_op jit(solution)/shard_map/ppermute | solution.py:252
  29.8 0.0 collective-permute-done.8.refs_2_
  29.8 1.1 %collective-permute-done.7.refs_1_ = f32[2,32,256]{2,1,0:T(8,128)S(1)} collective-permute-done((f32[2,32,256]{2,1,0:T(8,128)S(1)}, f32[2,32,256]{2,1,0:T(8,128)S(1)}, u32[]{:S(2)}, u32[]{:S(2)}) %collective-permute-start.7) | collective-permute-done | bytes 65568 | tf_op jit(solution)/shard_map/ppermute | solution.py:252
  30.9 0.8 %assemble.1 = f32[32,2048]{1,0:T(8,128)} custom-call(f32[2,32,256]{2,1,0:T(8,128)S(1)} %row_sweep.1.refs_0_, f32[2,32,256]{2,1,0:T(8,128)S(1)} %collective-permute-done.7.refs_1_, f32[2,32,256]{2,1,0:T(8,128)S(1)} %collective-permute-done.8.refs_2_, f32[2,32,256]{2,1,0:T(8,128)S(1)} %collective-permute-done.9.refs_3_), custom_call_target="tpu_custom_call" | custom-call | tf_op jit(solution)/shard_map/assemble/pallas_call | solution.py:19
  (1 shorter events, 0.0 us)
Async XLA Ops:
  0.0 7.5 %copy-start.1 = (f32[32,512]{1,0:T(8,128)S(1)}, f32[32,512]{1,0:T(8,128)}, u32[]{:S(2)}) copy-start(f32[32,512]{1,0:T(8,128)} %refs_0_.1) | copy-start | bytes 196612
  0.0 3.1 %collective-permute-start.2 = (f32[32,512]{1,0:T(8,128)}, f32[32,512]{1,0:T(8,128)S(1)}, u32[]{:S(2)}, u32[]{:S(2)}) collective-permute-start(f32[32,512]{1,0:T(8,128)} %refs_0_.1), channel_id=1, source_target_pairs={{0,1},{1,0},{2,3},{3,2},{4,5},{5,4},{6,7},{7,6},{8,9},{9,8},{10,11... | collective-permute-start | bytes 196616 | tf_op jit(solution)/shard_map/ppermute | solution.py:252
  0.5 6.4 %collective-permute-start.1 = (f32[32,512]{1,0:T(8,128)}, f32[32,512]{1,0:T(8,128)S(1)}, u32[]{:S(2)}, u32[]{:S(2)}) collective-permute-start(f32[32,512]{1,0:T(8,128)} %refs_0_.1), channel_id=1, source_target_pairs={{0,3},{1,2},{2,1},{3,0},{4,7},{5,6},{6,5},{7,4},{8,11},{9,10},{10,... | collective-permute-start | bytes 196616 | tf_op jit(solution)/shard_map/ppermute | solution.py:252
  3.1 4.5 %collective-permute-start = (f32[32,512]{1,0:T(8,128)}, f32[32,512]{1,0:T(8,128)S(1)}, u32[]{:S(2)}, u32[]{:S(2)}) collective-permute-start(f32[32,512]{1,0:T(8,128)} %refs_0_.1), channel_id=1, source_target_pairs={{0,2},{1,3},{2,0},{3,1},{4,6},{5,7},{6,4},{7,5},{8,10},{9,11},{10,... | collective-permute-start | bytes 196616 | tf_op jit(solution)/shard_map/ppermute | solution.py:252
  6.8 17.3 %copy-start = (f32[32,2048]{1,0:T(8,128)S(1)}, f32[32,2048]{1,0:T(8,128)}, u32[]{:S(2)}) copy-start(f32[32,2048]{1,0:T(8,128)} %refs_4_.1) | copy-start | bytes 786436
  8.9 6.0 %collective-permute-start.3 = (f32[264,128]{1,0:T(8,128)S(1)}, f32[264,128]{1,0:T(8,128)S(1)}, u32[]{:S(2)}, u32[]{:S(2)}) collective-permute-start(f32[264,128]{1,0:T(8,128)S(1)} %get-tuple-element.22), channel_id=1, source_target_pairs={{0,4},{4,0},{8,12},{12,8},{16,20},{20,16},{24,28},{28,24},{1,5},{5... | collective-permute-start | bytes 405512 | tf_op jit(solution)/shard_map/ppermute | solution.py:252
  15.0 5.5 %collective-permute-start.4 = (f32[136,128]{1,0:T(8,128)S(1)}, f32[136,128]{1,0:T(8,128)S(1)}, u32[]{:S(2)}, u32[]{:S(2)}) collective-permute-start(f32[136,128]{1,0:T(8,128)S(1)} %get-tuple-element.23), channel_id=1, source_target_pairs={{0,16},{4,20},{8,24},{12,28},{16,0},{20,4},{24,8},{28,12},{1,17},{... | collective-permute-start | bytes 208904 | tf_op jit(solution)/shard_map/ppermute | solution.py:252
  17.7 6.3 %collective-permute-start.5 = (f32[136,128]{1,0:T(8,128)S(1)}, f32[136,128]{1,0:T(8,128)S(1)}, u32[]{:S(2)}, u32[]{:S(2)}) collective-permute-start(f32[136,128]{1,0:T(8,128)S(1)} %get-tuple-element.24), channel_id=1, source_target_pairs={{0,24},{4,28},{8,16},{12,20},{16,8},{20,12},{24,0},{28,4},{1,25},{... | collective-permute-start | bytes 208904 | tf_op jit(solution)/shard_map/ppermute | solution.py:252
  19.0 5.1 %collective-permute-start.6 = (f32[136,128]{1,0:T(8,128)S(1)}, f32[136,128]{1,0:T(8,128)S(1)}, u32[]{:S(2)}, u32[]{:S(2)}) collective-permute-start(f32[136,128]{1,0:T(8,128)S(1)} %get-tuple-element.25), channel_id=1, source_target_pairs={{0,8},{4,12},{8,0},{12,4},{16,24},{20,28},{24,16},{28,20},{1,9},{5... | collective-permute-start | bytes 208904 | tf_op jit(solution)/shard_map/ppermute | solution.py:252
  24.6 5.2 %collective-permute-start.9 = (f32[2,32,256]{2,1,0:T(8,128)S(1)}, f32[2,32,256]{2,1,0:T(8,128)S(1)}, u32[]{:S(2)}, u32[]{:S(2)}) collective-permute-start(f32[2,32,256]{2,1,0:T(8,128)S(1)} %row_sweep.1.refs_0_), channel_id=1, source_target_pairs={{0,12},{4,8},{8,4},{12,0},{16,28},{20,24},{24,20},{28,16},{1,13},{... | collective-permute-start | bytes 196616 | tf_op jit(solution)/shard_map/ppermute | solution.py:252
  25.2 4.6 %collective-permute-start.8 = (f32[2,32,256]{2,1,0:T(8,128)S(1)}, f32[2,32,256]{2,1,0:T(8,128)S(1)}, u32[]{:S(2)}, u32[]{:S(2)}) collective-permute-start(f32[2,32,256]{2,1,0:T(8,128)S(1)} %row_sweep.1.refs_0_), channel_id=1, source_target_pairs={{0,8},{4,12},{8,0},{12,4},{16,24},{20,28},{24,16},{28,20},{1,9},{5... | collective-permute-start | bytes 196616 | tf_op jit(solution)/shard_map/ppermute | solution.py:252
  26.7 4.3 %collective-permute-start.7 = (f32[2,32,256]{2,1,0:T(8,128)S(1)}, f32[2,32,256]{2,1,0:T(8,128)S(1)}, u32[]{:S(2)}, u32[]{:S(2)}) collective-permute-start(f32[2,32,256]{2,1,0:T(8,128)S(1)} %row_sweep.1.refs_0_), channel_id=1, source_target_pairs={{0,4},{4,0},{8,12},{12,8},{16,20},{20,16},{24,28},{28,24},{1,5},{5... | collective-permute-start | bytes 196616 | tf_op jit(solution)/shard_map/ppermute | solution.py:252
